TPU v7x, 32 devices: a whole 2x2x4 slice. The times are simulated.
32 devices in a mesh: dp: 8 (over z, x), feat: 4 (over y, core).
Axes of the slice: x: 2, y: 2, z: 4, core: 2. Of those that a mesh axis runs over, the one named last changes fastest.
Arguments:
- tokens: bfloat16 [4096, 1024], P('dp'), may hold values from -6 to 6
- gain_one: float32 [1024], replicated, may hold values from 0.5 to 1.5
- w_query: bfloat16 [1024, 256], replicated, may hold values from -0.1875 to 0.1875
- w_key: bfloat16 [1024, 256], replicated, may hold values from -0.1875 to 0.1875
- w_value: bfloat16 [1024, 1024], replicated, may hold values from -0.1875 to 0.1875
- w_out: bfloat16 [1024, 1024], replicated, may hold values from -1.5 to 1.5
- gain_two: float32 [1024], replicated, may hold values from 0.5 to 1.5
- w_gate: bfloat16 [1024, 2752], P(None, 'feat'), may hold values from -0.1875 to 0.1875
- w_up: bfloat16 [1024, 2752], P(None, 'feat'), may hold values from -0.1875 to 0.1875
- w_down: bfloat16 [2752, 1024], P('feat'), may hold values from -0.109375 to 0.109375
- lengths: int32 [8, 4], P('dp'), may hold values from 0 to 512, as said below
- cotangent: bfloat16 [4096, 1024], P('dp'), may hold values from -6 to 6
Outputs:
- output: bfloat16 [4096, 1024], P('dp')
- grad_input: bfloat16 [4096, 1024], P('dp')
- grad_gain_one: float32 [1024], P('dp')
- grad_w_query: float32 [1024, 256], P('dp')
- grad_w_key: float32 [1024, 256], P('dp')
- grad_w_value: float32 [1024, 1024], P('dp')
- grad_w_out: float32 [1024, 1024], P('feat', 'dp')
- grad_gain_two: float32 [1024], P('dp')
- grad_w_gate: float32 [1024, 2752], P('dp', 'feat')
- grad_w_up: float32 [1024, 2752], P('dp', 'feat')
- grad_w_down: float32 [2752, 1024], P('feat', 'dp')
Inputs may be any that keep to these rules, and one draw needn't show every extreme that they name: `lengths`: row p lists the sequences packed from slot 0 of dp position p, in order; a row sums to at most 512, zeros are empty slots, and the slots after the sum are padding. One dp position holds a single sequence of 512 tokens.
All inputs are finite; a program needn't handle non-finite values.
Results may differ from a plain program's by a relative error of at most 0.023.
Values may be sent and summed in bfloat16 or wider, within the bound.
No kernel may reach another device: no remote copies, remote signals or barrier semaphores. Data moves between devices by JAX's collectives and lax.ppermute only.
A program may use at most 192 MiB of HBM per device.

v0:
```python
import math
import jax
import jax.numpy as jnp
from jax import lax
from jax.sharding import PartitionSpec as P

HEADS = 16
QK = 16
VD = 64
BLOCK = 512
EPSILON = 1e-05


def rms_factor(values):
    return lax.rsqrt(jnp.mean(values * values, axis=-1, keepdims=True) + EPSILON)


def norm_back(values, factor, gain_row, incoming):
    weighted = incoming * gain_row
    gain_grad = jnp.sum(incoming * values * factor, axis=0)
    value_grad = factor * weighted - values * factor * factor * factor * jnp.mean(
        weighted * values, axis=-1, keepdims=True
    )
    return (gain_grad, value_grad)


def split_parts(array):
    if array.dtype == jnp.bfloat16:
        return (array,)
    leading = array.astype(jnp.bfloat16)
    remainder = (array - leading.astype(jnp.float32)).astype(jnp.bfloat16)
    return (leading, remainder)


def exact_einsum(form, first, second):
    first_parts = split_parts(first)
    second_parts = split_parts(second)
    total = None
    for left_rank, left_part in enumerate(first_parts):
        for right_rank, right_part in enumerate(second_parts):
            if left_rank + right_rank < 2:
                term = jnp.einsum(form, left_part, right_part, preferred_element_type=jnp.float32)
                total = term if total is None else total + term
    return total


def feature_slice(projected, first_feature, slice_width, padded):
    row_count = projected.shape[0]
    split_heads = projected.reshape(row_count, -1, QK)
    heads_count = split_heads.shape[1]
    ones_part = jnp.ones((row_count, heads_count, 1), jnp.float32)
    linear = split_heads * QK ** (-0.25)
    square = (split_heads[:, :, :, None] * split_heads[:, :, None, :]).reshape(
        row_count, heads_count, QK * QK
    ) / math.sqrt(2.0 * QK)
    zeros_part = jnp.zeros((row_count, heads_count, padded - 1 - QK - QK * QK), jnp.float32)
    whole_map = jnp.concatenate([ones_part, linear, square, zeros_part], axis=2)
    return lax.dynamic_slice_in_dim(whole_map, first_feature, slice_width, 2)


def block_allowed(seg_block):
    places = jnp.arange(seg_block.shape[0], dtype=jnp.int32)
    return (places[:, None] >= places[None, :]) & (seg_block[:, None] == seg_block[None, :])


def segment_states(key_side, value_side, extra_side, seg_blocks, reverse):
    heads_count = key_side.shape[2]
    feature_count = key_side.shape[3]
    column_count = value_side.shape[3]

    def advance(carry_data, block_data):
        carried_state, carried_total, marker = carry_data
        key_block, value_block, extra_block, seg_block = block_data
        edge_segment = seg_block[0] if reverse else seg_block[-1]
        keep_state = (edge_segment == marker).astype(jnp.float32)
        chosen = seg_block == edge_segment
        key_selected = jnp.where(chosen[:, None, None], key_block, jnp.zeros_like(key_block))
        state_next = keep_state * carried_state + exact_einsum(
            "jhf,jhc->hfc", key_selected, value_block
        )
        total_next = keep_state * carried_total + exact_einsum(
            "jhf,jh->hf", key_selected, extra_block
        )
        return ((state_next, total_next, edge_segment), (carried_state, carried_total, marker))

    initial = (
        jnp.zeros((heads_count, feature_count, column_count), jnp.float32),
        jnp.zeros((heads_count, feature_count), jnp.float32),
        jnp.int32(-1),
    )
    _, entering = lax.scan(
        advance, initial, (key_side, value_side, extra_side, seg_blocks), reverse=reverse
    )
    return entering


def forward_block(inputs):
    query_block, key_block, value_block, seg_block, carried_state, carried_total, marker = inputs
    allowed = block_allowed(seg_block)
    scores = jnp.einsum("ihf,jhf->hij", query_block, key_block, preferred_element_type=jnp.float32)
    scores = jnp.where(allowed[None], scores, 0.0)
    numerator = exact_einsum("hij,jhc->ihc", scores, value_block)
    denominator = jnp.sum(scores, axis=2).T
    carried = (seg_block == marker).astype(jnp.float32)
    numerator = numerator + carried[:, None, None] * exact_einsum(
        "ihf,hfc->ihc", query_block, carried_state
    )
    denominator = denominator + carried[:, None] * exact_einsum(
        "ihf,hf->ih", query_block, carried_total
    )
    return (numerator, denominator)


def backward_block(inputs):
    (
        query_block,
        key_block,
        value_block,
        seg_block,
        grad_numer,
        grad_denom,
        carried_state,
        carried_total,
        marker,
        later_state,
        later_total,
        later_marker,
    ) = inputs
    allowed = block_allowed(seg_block)
    scores = jnp.einsum("ihf,jhf->hij", query_block, key_block, preferred_element_type=jnp.float32)
    scores = jnp.where(allowed[None], scores, 0.0)
    grad_scores = exact_einsum("ihc,jhc->hij", grad_numer, value_block) + grad_denom.T[:, :, None]
    grad_scores = jnp.where(allowed[None], grad_scores, 0.0)
    grad_query = exact_einsum("hij,jhf->ihf", grad_scores, key_block)
    grad_key = exact_einsum("hij,ihf->jhf", grad_scores, query_block)
    grad_value = exact_einsum("hij,ihc->jhc", scores, grad_numer)
    forward_on = (seg_block == marker).astype(jnp.float32)[:, None, None]
    grad_query = grad_query + forward_on * (
        exact_einsum("ihc,hfc->ihf", grad_numer, carried_state)
        + grad_denom[:, :, None] * carried_total[None]
    )
    later_on = (seg_block == later_marker).astype(jnp.float32)[:, None, None]
    grad_key = grad_key + later_on * (
        exact_einsum("jhc,hfc->jhf", value_block, later_state) + later_total[None]
    )
    grad_value = grad_value + later_on * exact_einsum("jhf,hfc->jhc", key_block, later_state)
    return (grad_query, grad_key, grad_value)


def local(
    tokens,
    gain_one,
    w_query,
    w_key,
    w_value,
    w_out,
    gain_two,
    w_gate,
    w_up,
    w_down,
    lengths,
    cotangent,
):
    token_count = tokens.shape[0]
    feat_count = lax.axis_size("feat")
    feat_index = lax.axis_index("feat")
    padded = (1 + QK + QK * QK + feat_count - 1) // feat_count * feat_count
    slice_width = padded // feat_count
    head_share = HEADS // feat_count
    column_share = head_share * VD
    block_count = token_count // BLOCK
    places = jnp.arange(token_count, dtype=jnp.int32)
    slots = jnp.arange(lengths.shape[1])
    bounds = jnp.sum(jnp.where(slots[None, :] <= slots[:, None], lengths[0][None, :], 0), axis=1)
    segments = jnp.sum((places[:, None] >= bounds[None, :]).astype(jnp.int32), axis=1)
    live_rows = (places < bounds[-1]).astype(jnp.float32)[:, None]

    def blocked(array):
        return array.reshape((block_count, BLOCK) + array.shape[1:])

    first_feature = feat_index * slice_width

    def make_features(projected):
        return feature_slice(projected, first_feature, slice_width, padded)

    inputs = tokens.astype(jnp.float32)
    scale_one = rms_factor(inputs)
    normed = (inputs * scale_one * gain_one).astype(jnp.bfloat16)
    queries = jnp.dot(normed, w_query, preferred_element_type=jnp.float32)
    key_rows = jnp.dot(normed, w_key, preferred_element_type=jnp.float32)
    values = jnp.dot(normed, w_value, preferred_element_type=jnp.float32).astype(jnp.bfloat16)
    query_feats = make_features(queries).astype(jnp.bfloat16)
    key_feats = make_features(key_rows).astype(jnp.bfloat16)
    value_heads = values.reshape(token_count, -1, VD)
    heads_here = value_heads.shape[1]
    seg_blocks = segments.reshape(block_count, BLOCK)
    query_blocks = blocked(query_feats)
    key_blocks = blocked(key_feats)
    value_blocks = blocked(value_heads)
    ones_extra = jnp.ones((block_count, BLOCK, heads_here), jnp.bfloat16)
    states, totals, markers = segment_states(
        key_blocks, value_blocks, ones_extra, seg_blocks, False
    )
    numerator, denominator = lax.map(
        forward_block, (query_blocks, key_blocks, value_blocks, seg_blocks, states, totals, markers)
    )
    numerator = numerator.reshape(token_count, heads_here * VD)
    denominator = denominator.reshape(token_count, heads_here)
    own_numer, own_denom = (
        lax.psum_scatter(numerator, "feat", scatter_dimension=1, tiled=True),
        lax.psum_scatter(denominator, "feat", scatter_dimension=1, tiled=True),
    )
    context_exact = own_numer.reshape(token_count, head_share, VD) / own_denom[:, :, None]
    context_low = context_exact.reshape(token_count, column_share).astype(jnp.bfloat16)
    out_rows = lax.dynamic_slice_in_dim(w_out, feat_index * column_share, column_share, 0)
    mixed_rows = jnp.dot(
        lax.all_gather(context_low, "feat", axis=1, tiled=True),
        w_out,
        preferred_element_type=jnp.float32,
    )
    residual = inputs + live_rows * mixed_rows
    scale_two = rms_factor(residual)
    normed_two = (residual * scale_two * gain_two).astype(jnp.bfloat16)
    gate_values = jnp.dot(normed_two, w_gate, preferred_element_type=jnp.float32)
    up_values = jnp.dot(normed_two, w_up, preferred_element_type=jnp.float32)
    gate_sigmoid = jax.nn.sigmoid(gate_values)
    activated = gate_values * gate_sigmoid
    inner_rows = (activated * up_values).astype(jnp.bfloat16)
    feed_rows = lax.psum(
        jnp.dot(inner_rows, w_down, preferred_element_type=jnp.float32).astype(jnp.bfloat16), "feat"
    ).astype(jnp.float32)
    output = (residual + live_rows * feed_rows).astype(jnp.bfloat16)
    grad_output = cotangent.astype(jnp.float32)
    grad_feed = (grad_output * live_rows).astype(jnp.bfloat16)
    grad_wdown = jnp.einsum("tf,td->fd", inner_rows, grad_feed, preferred_element_type=jnp.float32)
    grad_inner = jnp.dot(grad_feed, w_down.T, preferred_element_type=jnp.float32)
    grad_gate = (
        grad_inner * up_values * gate_sigmoid * (1.0 + gate_values * (1.0 - gate_sigmoid))
    ).astype(jnp.bfloat16)
    grad_upper = (grad_inner * activated).astype(jnp.bfloat16)
    grad_wgate = jnp.einsum("td,tf->df", normed_two, grad_gate, preferred_element_type=jnp.float32)
    grad_wup = jnp.einsum("td,tf->df", normed_two, grad_upper, preferred_element_type=jnp.float32)
    grad_normed_part = jnp.dot(grad_gate, w_gate.T, preferred_element_type=jnp.float32) + jnp.dot(
        grad_upper, w_up.T, preferred_element_type=jnp.float32
    )
    grad_normed_two = lax.psum(grad_normed_part.astype(jnp.bfloat16), "feat").astype(jnp.float32)
    grad_gain_second, grad_resid_norm = norm_back(residual, scale_two, gain_two, grad_normed_two)
    grad_residual = grad_output + grad_resid_norm
    grad_mixed = (live_rows * grad_residual).astype(jnp.bfloat16)
    grad_wout = jnp.einsum("tc,td->cd", context_low, grad_mixed, preferred_element_type=jnp.float32)
    grad_context = jnp.dot(grad_mixed, out_rows.T, preferred_element_type=jnp.float32).astype(
        jnp.bfloat16
    )
    grad_context_heads = grad_context.astype(jnp.float32).reshape(token_count, head_share, VD)
    grad_own_numer = grad_context_heads / own_denom[:, :, None]
    grad_own_denom = -jnp.sum(grad_context_heads * context_exact, axis=2) / own_denom
    grad_numer, grad_denom = (
        lax.all_gather(
            grad_own_numer.reshape(token_count, column_share).astype(jnp.bfloat16),
            "feat",
            axis=1,
            tiled=True,
        ).astype(jnp.float32),
        lax.all_gather(grad_own_denom.astype(jnp.bfloat16), "feat", axis=1, tiled=True).astype(
            grad_own_denom.dtype
        ),
    )
    grad_numer_blocks = blocked(grad_numer.reshape(token_count, heads_here, VD))
    grad_denom_blocks = blocked(grad_denom)
    later_states, later_totals, later_markers = segment_states(
        query_blocks, grad_numer_blocks, grad_denom_blocks, seg_blocks, True
    )
    grad_qfeat, grad_kfeat, grad_vpart = lax.map(
        backward_block,
        (
            query_blocks,
            key_blocks,
            value_blocks,
            seg_blocks,
            grad_numer_blocks,
            grad_denom_blocks,
            states,
            totals,
            markers,
            later_states,
            later_totals,
            later_markers,
        ),
    )
    _, query_pull = jax.vjp(make_features, queries)
    _, key_pull = jax.vjp(make_features, key_rows)
    grad_query_part = query_pull(grad_qfeat.reshape(token_count, heads_here, slice_width))[0]
    grad_key_part = key_pull(grad_kfeat.reshape(token_count, heads_here, slice_width))[0]
    grad_value_part = grad_vpart.reshape(token_count, heads_here * VD)
    summed_query, summed_key, summed_value = (
        lax.psum(grad_query_part.astype(jnp.bfloat16), "feat").astype(jnp.float32),
        lax.psum(grad_key_part.astype(jnp.bfloat16), "feat").astype(jnp.float32),
        lax.psum(grad_value_part.astype(jnp.bfloat16), "feat").astype(jnp.float32),
    )
    grad_queries = summed_query.astype(jnp.bfloat16)
    grad_keys = summed_key.astype(jnp.bfloat16)
    grad_values = summed_value.astype(jnp.bfloat16)
    grad_wquery = jnp.einsum("td,tk->dk", normed, grad_queries, preferred_element_type=jnp.float32)
    grad_wkey = jnp.einsum("td,tk->dk", normed, grad_keys, preferred_element_type=jnp.float32)
    grad_wvalue = jnp.einsum("td,tk->dk", normed, grad_values, preferred_element_type=jnp.float32)
    grad_normed = (
        jnp.dot(grad_queries, w_query.T, preferred_element_type=jnp.float32)
        + jnp.dot(grad_keys, w_key.T, preferred_element_type=jnp.float32)
        + jnp.dot(grad_values, w_value.T, preferred_element_type=jnp.float32)
    )
    grad_gain_first, grad_input_norm = norm_back(inputs, scale_one, gain_one, grad_normed)
    grad_input = (grad_residual + grad_input_norm).astype(jnp.bfloat16)
    summed_all = (
        lax.psum_scatter(
            grad_wquery.astype(jnp.bfloat16), "dp", scatter_dimension=0, tiled=True
        ).astype(jnp.float32),
        lax.psum_scatter(
            grad_wkey.astype(jnp.bfloat16), "dp", scatter_dimension=0, tiled=True
        ).astype(jnp.float32),
        lax.psum_scatter(
            grad_wvalue.astype(jnp.bfloat16), "dp", scatter_dimension=0, tiled=True
        ).astype(jnp.float32),
        lax.psum_scatter(
            grad_wout.astype(jnp.bfloat16), "dp", scatter_dimension=1, tiled=True
        ).astype(jnp.float32),
        lax.psum_scatter(
            grad_gain_first.astype(jnp.bfloat16), "dp", scatter_dimension=0, tiled=True
        ).astype(jnp.float32),
        lax.psum_scatter(
            grad_wgate.astype(jnp.bfloat16), "dp", scatter_dimension=0, tiled=True
        ).astype(jnp.float32),
        lax.psum_scatter(
            grad_wup.astype(jnp.bfloat16), "dp", scatter_dimension=0, tiled=True
        ).astype(jnp.float32),
        lax.psum_scatter(
            grad_wdown.astype(jnp.bfloat16), "dp", scatter_dimension=1, tiled=True
        ).astype(jnp.float32),
        lax.psum_scatter(
            grad_gain_second.astype(jnp.bfloat16), "dp", scatter_dimension=0, tiled=True
        ).astype(jnp.float32),
    )
    (
        sum_query,
        sum_key,
        sum_value,
        sum_out,
        sum_gain_first,
        sum_gate,
        sum_up,
        sum_down,
        sum_gain_second,
    ) = summed_all
    return (
        output,
        grad_input,
        sum_gain_first,
        sum_query,
        sum_key,
        sum_value,
        sum_out,
        sum_gain_second,
        sum_gate,
        sum_up,
        sum_down,
    )


def solution(mesh):
    in_specs = (
        P("dp", None),
        P(),
        P(),
        P(),
        P(),
        P(),
        P(),
        P(None, "feat"),
        P(None, "feat"),
        P("feat", None),
        P("dp", None),
        P("dp", None),
    )
    out_specs = (
        P("dp", None),
        P("dp", None),
        P("dp"),
        P("dp", None),
        P("dp", None),
        P("dp", None),
        P("feat", "dp"),
        P("dp"),
        P("dp", "feat"),
        P("dp", "feat"),
        P("feat", "dp"),
    )
    return jax.shard_map(local, mesh=mesh, in_specs=in_specs, out_specs=out_specs, check_vma=False)
```

profile of v0, /device:TPU:0, one launch (start us, length us, event | category | flops | bytes accessed | tf_op | source)
XLA Modules:
  0.0 863.3 jit_solution(11175286774580664384)
XLA Ops:
  9.1 3.5 convolution_convert_fusion.5
  12.6 2.4 copy.63
  15.4 2.3 broadcast_multiply_fusion
  18.6 3.2 multiply_multiply_fusion
  27.6 3.1 select_reduce_fusion
  32.4 4.1 copy-done.1
  36.5 2.5 fusion.36
  39.0 1.8 multiply_add_fusion
  44.4 14.1 %all-reduce = f32[512,16]{0,1:T(8,128)} all-reduce(f32[512,16]{0,1:T(8,128)} %fusion.55), channel_id=3, replica_groups=mesh['dp'=8,'feat'=4] {'feat'}, use_global_device_ids=true, to_apply=%region_5.6.clone | all-reduce | flops 8192 | bytes 65536
  59.2 15.9 %reduce-scatter.17.cloned.1.call-done = f32[512,256]{0,1:T(8,128)} async-done(((f32[512,1024]{0,1:T(8,128)}), f32[512,256]{0,1:T(8,128)}) %reduce-scatter.17.cloned.1.call-update) | async-done | bytes 524304 | tf_op jit(solution)/shard_map/reduce_scatter | solution.py:210
  75.1 1.8 fusion.38
  78.2 15.9 %all-gather.4.cloned.1.call-done = bf16[512,1024]{0,1:T(8,128)(2,1)} async-done(((bf16[512,256]{0,1:T(8,128)(2,1)}), bf16[512,1024]{0,1:T(8,128)(2,1)}) %all-gather.4.cloned.1.call-update) | async-done | bytes 1048592 | tf_op jit(solution)/shard_map/all_gather | solution.py:217
  94.1 3.6 multiply_reduce_fusion.4
  103.2 2.5 multiply_convert_fusion.2
  106.8 2.0 add_convert_fusion.1
  108.9 36.2 %all-reduce.8.cloned.1.call-done = bf16[512,1024]{1,0:T(8,128)(2,1)} async-done(((bf16[512,1024]{1,0:T(8,128)(2,1)}), bf16[512,1024]{1,0:T(8,128)(2,1)}) %all-reduce.8.cloned.1.call-update) | async-done | bytes 1048592 | tf_op jit(solution)/shard_map/psum | solution.py:246
  145.1 3.3 fusion.24
  148.5 2.0 convert_add_fusion.1
  151.8 2.5 fusion.39
  154.4 3.6 convolution_convert_fusion.4
  158.9 6.0 all-gather
  167.6 4.0 all-gather.6.cloned.1.call-done
  171.6 10.2 %fusion.35 = f32[16,64,512]{2,1,0:T(8,128)} fusion(bf16[512,16,64]{0,2,1:T(8,128)(2,1)} %bitcast.117, f32[16,512,512]{1,2,0:T(8,128)} %copy-done.1, pred[512,512]{0,1:T(8,128)(4,1)S(1)} %fusion.31), kind=kOutput, calls=%fused_computation.87 | convolution fusion | flops 557842432 | bytes 20185088 | tf_op jit(solution)/shard_map/while/body/eval_jaxpr/hij,ihc->jhc/dot_general | solution.py:42
  181.8 9.8 %fusion.33 = f32[16,64,512]{2,1,0:T(8,128)} fusion(bf16[512,16,64]{0,2,1:T(8,128)(2,1)S(1)} %bitcast.118, f32[16,512,512]{1,2,0:T(8,128)} %copy-done.1, pred[512,512]{0,1:T(8,128)(4,1)S(1)} %fusion.31), kind=kOutput, calls=%fused_computation.85 | convolution fusion | flops 541065216 | bytes 20185088 | tf_op jit(solution)/shard_map/while/body/eval_jaxpr/hij,ihc->jhc/dot_general | solution.py:42
  191.6 9.7 %fusion.32 = f32[16,64,512]{2,1,0:T(8,128)} fusion(f32[16,512,512]{1,2,0:T(8,128)} %copy-done.1, pred[512,512]{0,1:T(8,128)(4,1)S(1)} %fusion.31, bf16[512,16,64]{0,2,1:T(8,128)(2,1)S(1)} %bitcast.119), kind=kOutput, calls=%fused_computation.84 | convolution fusion | flops 542638080 | bytes 20185088 | tf_op jit(solution)/shard_map/while/body/eval_jaxpr/hij,ihc->jhc/dot_general | solution.py:42
  201.3 1.9 fusion.37
  203.2 8.1 fusion.90
  211.3 11.0 %add_select_fusion = f32[16,512,512]{1,2,0:T(8,128)} fusion(f32[16,512,512]{1,2,0:T(8,128)} %fusion.90, bf16[512,16,64]{0,2,1:T(8,128)(2,1)S(1)} %bitcast.127, f32[16,512]{1,0:T(8,128)S(1)} %copy-done.37, pred[512,512]{0,1:T(8,128)(4,1)S(1)} %fusion.31, bf16[512,16,64]{0,2,1:T(8,128)(2,1)S(1)} %bitcast.122), kind=kOutput, calls=%fused_computation.1 | convolution fusion | flops 551026688 | bytes 35946496 | tf_op jit(solution)/shard_map/while/body/eval_jaxpr/ihc,jhc->hij/dot_general | solution.py:42
  222.4 9.0 %fusion.64 = f32[16,69,512]{2,1,0:T(8,128)} fusion(bf16[512,16,69]{0,2,1:T(8,128)(2,1)S(1)} %copy-done.13, f32[16,512,512]{1,2,0:T(8,128)} %add_select_fusion), kind=kOutput, calls=%fused_computation.138 | convolution fusion | flops 583008256 | bytes 20168704 | tf_op jit(solution)/shard_map/while/body/eval_jaxpr/hij,jhf->ihf/dot_general | solution.py:42
  231.4 2.4 copy-done.2
  233.8 3.0 fusion.67
  236.7 9.9 %fusion.62 = f32[16,69,512]{2,1,0:T(8,128)} fusion(bf16[512,16,69]{0,2,1:T(8,128)(2,1)S(1)} %get-tuple-element.138, f32[16,512,512]{1,2,0:T(8,128)} %add_select_fusion), kind=kOutput, calls=%fused_computation.136 | convolution fusion | flops 583008256 | bytes 20168704 | tf_op jit(solution)/shard_map/while/body/eval_jaxpr/hij,ihf->jhf/dot_general | solution.py:42
  246.6 14.8 %fusion.66 = f32[16,69,512]{2,1,0:T(8,128)} fusion(bf16[512,16,69]{0,2,1:T(8,128)(2,1)S(1)} %get-tuple-element.138, f32[16,512,512]{1,2,0:T(8,128)} %add_select_fusion), kind=kOutput, calls=%fused_computation.140 | convolution fusion | flops 595591168 | bytes 20168704 | tf_op jit(solution)/shard_map/while/body/eval_jaxpr/hij,ihf->jhf/dot_general | solution.py:42
  261.4 2.2 fusion.13
  263.6 4.8 broadcast.180.clone
  268.4 11.4 %dynamic_update_slice.34 = f32[512,16,276]{0,2,1:T(8,128)} dynamic-update-slice(f32[512,16,276]{0,2,1:T(8,128)} %broadcast.180.clone, f32[512,16,69]{0,2,1:T(8,128)} %fusion.13, s32[]{:T(128)} %constant.119.clone.1, s32[]{:T(128)} %constant.119.clone.1, s32[]{:T(128)S(6)} %select_n.30) | dynamic-update-slice | bytes 4521988 | tf_op jit(solution)/shard_map/transpose(jvp())/dynamic_update_slice | solution.py:58
  279.8 4.8 slice_multiply_fusion.1
  285.9 5.7 multiply_reduce_fusion.2
  291.7 1.9 add_bitcast_fusion
  293.6 4.7 broadcast.180.clone.1
  298.3 11.4 %dynamic_update_slice.35 = f32[512,16,276]{0,2,1:T(8,128)} dynamic-update-slice(f32[512,16,276]{0,2,1:T(8,128)} %broadcast.180.clone.1, f32[512,16,69]{0,2,1:T(8,128)} %add_bitcast_fusion, s32[]{:T(128)} %constant.119.clone.1, s32[]{:T(128)} %constant.119.clone.1, s32[]{:T(128)S(6)} %select_n.30) | dynamic-update-slice | bytes 4521988 | tf_op jit(solution)/shard_map/transpose(jvp())/dynamic_update_slice | solution.py:58
  309.7 4.8 slice_multiply_fusion
  315.9 5.5 multiply_reduce_fusion
  321.4 2.2 fusion.43
  324.6 1.8 add_convert_fusion
  327.3 2.1 convolution_convert_fusion.6
  330.4 2.4 convolution_convert_fusion.2
  334.4 2.3 convolution_convert_fusion.1
  338.7 3.6 convolution_convert_fusion.3
  342.3 2.7 copy.94
  345.0 42.0 %all-reduce.10.cloned.1.call-done = (bf16[512,1024]{1,0:T(8,128)(2,1)}, bf16[512,1024]{0,1:T(8,128)(2,1)}, bf16[512,256]{0,1:T(8,128)(2,1)}, bf16[512,256]{0,1:T(8,128)(2,1)}) async-done(((bf16[512,1024]{1,0:T(8,128)(2,1)}, bf16[512,1024]{0,1:T(8,128)(2,1)}, bf16[512,256]{0,1:T(8,128)(2,1)}, bf16[512,256]{0,1:T(8,128)(2,1)}), (bf16[512,1024]{1,0:T(8,128)(2,1)}, bf16[512,1024]{0,1:T(8,128)(2,1)}, ...) | async-done | bytes 2621456 | tf_op jit(solution)/shard_map/psum | solution.py:229
  387.0 2.4 convolution_convert_fusion.8
  391.1 4.0 convolution_convert_fusion
  397.0 55.2 %reduce-scatter.25.cloned.1.call-done = bf16[128,256]{1,0:T(8,128)(2,1)} async-done(((bf16[1024,256]{1,0:T(8,128)(2,1)}), bf16[128,256]{1,0:T(8,128)(2,1)}) %reduce-scatter.25.cloned.1.call-update) | async-done | bytes 65552
  453.8 66.0 %reduce-scatter.27.cloned.1.call-done = bf16[128,688]{1,0:T(8,128)(2,1)} async-done(((bf16[1024,688]{1,0:T(8,128)(2,1)}), bf16[128,688]{1,0:T(8,128)(2,1)}) %reduce-scatter.27.cloned.1.call-update) | async-done | bytes 176144
  521.7 65.4 %reduce-scatter.29.cloned.1.call-done = bf16[128,688]{1,0:T(8,128)(2,1)} async-done(((bf16[1024,688]{1,0:T(8,128)(2,1)}), bf16[128,688]{1,0:T(8,128)(2,1)}) %reduce-scatter.29.cloned.1.call-update) | async-done | bytes 176144
  589.0 65.8 %reduce-scatter.31.cloned.1.call-done = bf16[128,688]{1,0:T(8,128)(2,1)} async-done(((bf16[1024,688]{1,0:T(8,128)(2,1)}), bf16[128,688]{1,0:T(8,128)(2,1)}) %reduce-scatter.31.cloned.1.call-update) | async-done | bytes 176144
  659.6 2.3 fusion.28
  661.9 19.3 %all-reduce.3 = (bf16[1024]{0:T(1024)(128)(2,1)S(1)}, bf16[1024]{0:T(1024)(128)(2,1)S(1)}) all-reduce(bf16[1024]{0:T(1024)(128)(2,1)S(1)} %get-tuple-element.111, bf16[1024]{0:T(1024)(128)(2,1)S(1)} %copy-done.48), channel_id=4, replica_groups=mesh['dp'=8,'feat'=4] {'dp'}, use_global_device_ids=true, to_apply=%region_20.21.clone | all-reduce | flops 2048 | bytes 8192
  681.9 5.3 fusion.19
  687.2 32.2 %reduce-scatter.19.cloned.1.call-done = bf16[128,256]{1,0:T(8,128)(2,1)} async-done(((bf16[1024,256]{1,0:T(8,128)(2,1)}), bf16[128,256]{1,0:T(8,128)(2,1)}) %reduce-scatter.19.cloned.1.call-update) | async-done | bytes 65552 | tf_op jit(solution)/shard_map/reduce_scatter | solution.py:314
  720.9 63.2 %reduce-scatter.21.cloned.1.call-done = bf16[128,256]{1,0:T(8,128)(2,1)} async-done(((bf16[1024,256]{1,0:T(8,128)(2,1)}), bf16[128,256]{1,0:T(8,128)(2,1)}) %reduce-scatter.21.cloned.1.call-update) | async-done | bytes 65552 | tf_op jit(solution)/shard_map/reduce_scatter | solution.py:317
  785.6 68.6 %reduce-scatter.23.cloned.1.call-done = bf16[128,1024]{1,0:T(8,128)(2,1)} async-done(((bf16[1024,1024]{1,0:T(8,128)(2,1)}), bf16[128,1024]{1,0:T(8,128)(2,1)}) %reduce-scatter.23.cloned.1.call-update) | async-done | bytes 262160 | tf_op jit(solution)/shard_map/reduce_scatter | solution.py:320
  854.2 1.8 convert_element_type.328
  (192 shorter events, 52.8 us)
Async XLA Ops:
  7.2 1.9 copy-start
  7.2 67.9 %reduce-scatter.17.cloned.1.call-start = ((), (), s32[]{:S(2)}) async-start(), calls=%async_computation.8 | async-start | bytes 2621440 | tf_op jit(solution)/shard_map/reduce_scatter | solution.py:210
  9.1 12.8 %copy-start.44 = (f32[512]{0:T(512)}, f32[512]{0:T(512)S(1)}, u32[]{:S(2)}) copy-start(f32[512]{0:T(512)S(1)} %add_rsqrt_fusion.1) | copy-start | bytes 6148
  12.6 2.4 copy-start.55
  12.6 2.8 copy-start.16
  12.6 2.8 copy-start.46
  15.1 6.7 copy-start.49
  23.6 1.4 copy-start.28
  23.6 2.4 copy-start.15
  23.6 2.4 copy-start.38
  27.6 3.1 copy-start.12
  27.6 3.1 copy-start.8
  30.7 5.8 copy-start.1
  40.8 36.2 %copy-start.50 = (s32[4]{0:T(128)S(1)}, s32[4]{0:T(128)}, u32[]{:S(2)}) copy-start(s32[4]{0:T(128)} %copy-done.49) | copy-start | bytes 52
  40.9 53.2 %all-gather.4.cloned.1.call-start = ((), (), s32[]{:S(2)}) async-start(), calls=%async_computation.9 | async-start | bytes 1310720 | tf_op jit(solution)/shard_map/all_gather | solution.py:217
  76.9 68.2 %all-reduce.8.cloned.1.call-start = ((), (), s32[]{:S(2)}) async-start(), calls=%async_computation.10 | async-start | bytes 2097152 | tf_op jit(solution)/shard_map/psum | solution.py:246
  94.1 3.7 copy-start.42
  97.7 3.1 copy-start.5
  97.7 2.1 copy-start.51
  99.8 1.7 copy-start.52
  101.5 1.2 copy-start.35
  101.6 1.7 copy-start.53
  108.8 62.7 %all-gather.6.cloned.1.call-start = ((), (), s32[]{:S(2)}) async-start(), calls=%async_computation.11 | async-start | bytes 1310720 | tf_op jit(solution)/shard_map/all_gather | solution.py:258
  145.1 3.3 copy-start.6
  145.1 3.3 copy-start.30
  150.5 1.3 copy-start.11
  154.3 232.7 %all-reduce.10.cloned.1.call-start = ((), (), s32[]{:S(2)}) async-start(), calls=%async_computation.19 | async-start | bytes 5242880 | tf_op jit(solution)/shard_map/psum | solution.py:229
  154.4 3.6 copy-start.32
  154.4 3.6 copy-start.33
  171.6 10.2 %copy-start.7 = (bf16[512,1024]{0,1:T(8,128)(2,1)S(1)}, bf16[512,1024]{0,1:T(8,128)(2,1)}, u32[]{:S(2)}) copy-start(bf16[512,1024]{0,1:T(8,128)(2,1)} %all-gather.6.cloned.1.call-done) | copy-start | bytes 3145732
  201.3 1.9 copy-start.9
  203.2 8.1 copy-start.37
  211.3 11.0 %copy-start.13 = (bf16[512,16,69]{0,2,1:T(8,128)(2,1)S(1)}, bf16[512,16,69]{0,2,1:T(8,128)(2,1)}, u32[]{:S(2)}) copy-start(bf16[512,16,69]{0,2,1:T(8,128)(2,1)} %copy-done.12) | copy-start | bytes 3391492
  222.4 11.4 %copy-start.2 = (f32[16,512,512]{1,2,0:T(8,128)S(1)}, f32[16,512,512]{1,2,0:T(8,128)}, u32[]{:S(2)}) copy-start(f32[16,512,512]{1,2,0:T(8,128)} %add_select_fusion) | copy-start | bytes 50331652
  246.6 14.8 %copy-start.20 = (f32[16,69,512]{2,1,0:T(8,128)S(1)}, f32[16,69,512]{2,1,0:T(8,128)}, u32[]{:S(2)}) copy-start(f32[16,69,512]{2,1,0:T(8,128)} %fusion.64) | copy-start | bytes 6782980
  246.6 14.8 %copy-start.21 = (f32[16,69,512]{2,1,0:T(8,128)S(1)}, f32[16,69,512]{2,1,0:T(8,128)}, u32[]{:S(2)}) copy-start(f32[16,69,512]{2,1,0:T(8,128)} %fusion.67) | copy-start | bytes 6782980
  246.6 14.8 %copy-start.22 = (f32[16,69,512]{2,1,0:T(8,128)S(1)}, f32[16,69,512]{2,1,0:T(8,128)}, u32[]{:S(2)}) copy-start(f32[16,69,512]{2,1,0:T(8,128)} %fusion.37) | copy-start | bytes 6782980
  246.6 14.8 %copy-start.41 = (f32[512,16]{0,1:T(8,128)S(1)}, f32[512,16]{0,1:T(8,128)}, u32[]{:S(2)}) copy-start(f32[512,16]{0,1:T(8,128)} %multiply_bitcast_fusion) | copy-start | bytes 98308
  279.8 6.1 copy-start.4
  279.8 6.1 copy-start.29
  285.9 5.7 copy-start.10
  285.9 5.7 copy-start.18
  285.9 5.7 copy-start.19
  309.7 6.1 copy-start.3
  309.7 6.1 copy-start.27
  315.9 8.7 %copy-start.24 = (f32[16,64,512]{2,1,0:T(8,128)S(1)}, f32[16,64,512]{2,1,0:T(8,128)}, u32[]{:S(2)}) copy-start(f32[16,64,512]{2,1,0:T(8,128)} %fusion.33) | copy-start | bytes 6291460
  315.9 8.7 %copy-start.25 = (f32[16,64,512]{2,1,0:T(8,128)S(1)}, f32[16,64,512]{2,1,0:T(8,128)}, u32[]{:S(2)}) copy-start(f32[16,64,512]{2,1,0:T(8,128)} %fusion.32) | copy-start | bytes 6291460
  321.4 3.2 copy-start.14
  321.4 3.1 copy-start.23
  326.3 125.9 %reduce-scatter.25.cloned.1.call-start = ((), (), s32[]{:S(2)}) async-start(), calls=%async_computation.15 | async-start | bytes 589824
  330.4 189.5 %reduce-scatter.27.cloned.1.call-start = ((), (), s32[]{:S(2)}) async-start(), calls=%async_computation.16 | async-start | bytes 1769472
  334.4 252.7 %reduce-scatter.29.cloned.1.call-start = ((), (), s32[]{:S(2)}) async-start(), calls=%async_computation.17 | async-start | bytes 1769472
  338.4 316.4 %reduce-scatter.31.cloned.1.call-start = ((), (), s32[]{:S(2)}) async-start(), calls=%async_computation.18 | async-start | bytes 1769472
  342.3 44.8 %copy-start.17 = (bf16[512,1024]{1,0:T(8,128)(2,1)S(1)}, bf16[512,1024]{1,0:T(8,128)(2,1)}, u32[]{:S(2)}) copy-start(bf16[512,1024]{1,0:T(8,128)(2,1)} %param.12) | copy-start | bytes 3145732
  342.3 44.8 %copy-start.45 = (f32[512]{0:T(512)S(1)}, f32[512]{0:T(512)}, u32[]{:S(2)}) copy-start(f32[512]{0:T(512)} %copy-done.44) | copy-start | bytes 6148
  342.3 44.8 %copy-start.47 = (f32[1024]{0:T(1024)S(1)}, f32[1024]{0:T(1024)}, u32[]{:S(2)}) copy-start(f32[1024]{0:T(1024)} %param.13) | copy-start | bytes 12292
  345.0 374.4 %reduce-scatter.19.cloned.1.call-start = ((), (), s32[]{:S(2)}) async-start(), calls=%async_computation.12 | async-start | bytes 589824 | tf_op jit(solution)/shard_map/reduce_scatter | solution.py:314
  387.0 2.5 copy-start.39
  389.5 394.6 %reduce-scatter.21.cloned.1.call-start = ((), (), s32[]{:S(2)}) async-start(), calls=%async_computation.13 | async-start | bytes 589824 | tf_op jit(solution)/shard_map/reduce_scatter | solution.py:317
  391.0 463.2 %reduce-scatter.23.cloned.1.call-start = ((), (), s32[]{:S(2)}) async-start(), calls=%async_computation.14 | async-start | bytes 2359296 | tf_op jit(solution)/shard_map/reduce_scatter | solution.py:320
  655.9 2.4 copy-start.54
  658.3 1.3 copy-start.36
  658.3 1.3 copy-start.40
  659.6 2.3 copy-start.48
  (8 other events, 6.8 us)
Sparse Core Ops, SparseCore 0:
  41.0 34.0 reduce-scatter.16
  77.3 16.7 all-gather.3
  109.0 36.1 all-reduce.7
  154.4 17.0 all-gather.5
  326.5 60.5 all-reduce.9
  390.2 61.9 reduce-scatter.24
  456.0 63.7 reduce-scatter.26
  523.3 63.8 reduce-scatter.28
  590.9 63.8 reduce-scatter.30
  658.6 60.7 reduce-scatter.18
  723.1 60.9 reduce-scatter.20
  787.5 66.7 reduce-scatter.22
where the time goes:
time: 875 us; the launch traced here: 863 us
  waiting for transfers between devices  531 us (61%)
  matrix products  151 us (17%)
  local copies, waits for them, and re-layouts  67.8 us (8%)
  other arithmetic  57.4 us (7%)
  blocking collectives  39.5 us (5%)
  between operations  16.5 us (2%)
    unnamed x16, waiting for transfers between devices  253 us
    dot_general x17, matrix products, exact_einsum(): jnp.einsum(form, left_part, right_part, preferred_element_type=jnp.float32)  99.6 us
    reduce_scatter x1, waiting for transfers between devices, local(): lax.psum_scatter(grad_wvalue.astype(jnp.bfloat16), 'dp', scatter_dimensio...  68.6 us
    reduce_scatter x1, waiting for transfers between devices, local(): lax.psum_scatter(grad_wkey.astype(jnp.bfloat16), 'dp', scatter_dimension=...  63.2 us
    psum x1, waiting for transfers between devices, local(): lax.psum(jnp.dot(inner_rows, w_down, preferred_element_type=jnp.float32)....  42 us
    psum x1, waiting for transfers between devices, local(): lax.psum(grad_normed_part.astype(jnp.bfloat16), 'feat').astype(jnp.float32)  36.2 us
    unnamed x2, blocking collectives  33.4 us
    reduce_scatter x1, waiting for transfers between devices, local(): lax.psum_scatter(grad_wquery.astype(jnp.bfloat16), 'dp', scatter_dimensio...  32.2 us
  transfers between devices with their start and end apart: 12, of which 12 were waited for; matrix products, arithmetic and copies ran while one was open for 7% of the time, Pallas kernels for 0%

commit v1 on v0

--- a/solution.py
+++ b/solution.py
@@ -9,6 +9,10 @@
 VD = 64
 BLOCK = 512
 EPSILON = 1e-05
+
+
+def advance_the_squares(content):
+    return lax.all_gather(content, "feat").sum(axis=0)
 
 
 def rms_factor(values):
@@ -243,7 +247,7 @@
     grad_normed_part = jnp.dot(grad_gate, w_gate.T, preferred_element_type=jnp.float32) + jnp.dot(
         grad_upper, w_up.T, preferred_element_type=jnp.float32
     )
-    grad_normed_two = lax.psum(grad_normed_part.astype(jnp.bfloat16), "feat").astype(jnp.float32)
+    grad_normed_two = advance_the_squares(grad_normed_part.astype(jnp.bfloat16)).astype(jnp.float32)
     grad_gain_second, grad_resid_norm = norm_back(residual, scale_two, gain_two, grad_normed_two)
     grad_residual = grad_output + grad_resid_norm
     grad_mixed = (live_rows * grad_residual).astype(jnp.bfloat16)

time: 875 us -> 878 us (level)
    psum x1 -> x0, waiting for transfers between devices: 36.2 us -> none  [local(): lax.psum(grad_normed_part.astype(jnp.bfloat16), 'feat').astype(jnp.float32)]
    all_gather x0 -> x1, waiting for transfers between devices: none -> 34.6 us  [advance_the_squares(): return lax.all_gather(content, 'feat').sum(axis=0)]
    unnamed x131 -> x135, local copies, waits for them, and re-layouts: 31 us -> 31.1 us
where the time goes in v1:
time: 878 us; the launch traced here: 866 us
  waiting for transfers between devices  528 us (60%)
  matrix products  152 us (17%)
  local copies, waits for them, and re-layouts  67.9 us (8%)
  other arithmetic  61.8 us (7%)
  blocking collectives  39.6 us (5%)
  between operations  16.5 us (2%)
    unnamed x16, waiting for transfers between devices  252 us
    dot_general x17, matrix products, exact_einsum(): jnp.einsum(form, left_part, right_part, preferred_element_type=jnp.float32)  99.6 us
    reduce_scatter x1, waiting for transfers between devices, local(): lax.psum_scatter(grad_wvalue.astype(jnp.bfloat16), 'dp', scatter_dimensio...  69.1 us
    reduce_scatter x1, waiting for transfers between devices, local(): lax.psum_scatter(grad_wkey.astype(jnp.bfloat16), 'dp', scatter_dimension=...  62.7 us
    psum x1, waiting for transfers between devices, local(): lax.psum(jnp.dot(inner_rows, w_down, preferred_element_type=jnp.float32)....  40.9 us
    all_gather x1, waiting for transfers between devices, advance_the_squares(): return lax.all_gather(content, 'feat').sum(axis=0)  34.6 us
    unnamed x2, blocking collectives  33.6 us
    reduce_scatter x1, waiting for transfers between devices, local(): lax.psum_scatter(grad_wquery.astype(jnp.bfloat16), 'dp', scatter_dimensio...  32.8 us
  transfers between devices with their start and end apart: 12, of which 12 were waited for; matrix products, arithmetic and copies ran while one was open for 7% of the time, Pallas kernels for 0%

profile of v1, /device:TPU:0, one launch (start us, length us, event | category | flops | bytes accessed | tf_op | source)
XLA Modules:
  0.0 866.0 jit_solution(1422163268915153997)
XLA Ops:
  9.1 3.5 convolution_convert_fusion.5
  12.6 2.4 copy.63
  15.4 2.3 broadcast_multiply_fusion
  18.6 3.2 multiply_multiply_fusion
  27.6 3.1 select_reduce_fusion
  32.3 4.1 copy-done.1
  36.5 2.5 fusion.36
  39.0 1.8 multiply_add_fusion
  44.4 14.1 %all-reduce = f32[512,16]{0,1:T(8,128)} all-reduce(f32[512,16]{0,1:T(8,128)} %fusion.55), channel_id=4, replica_groups=mesh['dp'=8,'feat'=4] {'feat'}, use_global_device_ids=true, to_apply=%region_5.6.clone | all-reduce | flops 8192 | bytes 65536
  59.2 15.9 %reduce-scatter.17.cloned.1.call-done = f32[512,256]{0,1:T(8,128)} async-done(((f32[512,1024]{0,1:T(8,128)}), f32[512,256]{0,1:T(8,128)}) %reduce-scatter.17.cloned.1.call-update) | async-done | bytes 524304 | tf_op jit(solution)/shard_map/reduce_scatter | solution.py:214
  78.2 15.9 %all-gather.6.cloned.1.call-done = bf16[512,1024]{0,1:T(8,128)(2,1)} async-done(((bf16[512,256]{0,1:T(8,128)(2,1)}), bf16[512,1024]{0,1:T(8,128)(2,1)}) %all-gather.6.cloned.1.call-update) | async-done | bytes 1048592 | tf_op jit(solution)/shard_map/all_gather | solution.py:221
  94.1 3.6 multiply_reduce_fusion.4
  103.2 2.5 multiply_convert_fusion.2
  106.8 2.0 add_convert_fusion.1
  108.9 34.6 %all-gather.10.cloned.1.call-done = bf16[2048,1024]{1,0:T(8,128)(2,1)} async-done(((bf16[512,1024]{1,0:T(8,128)(2,1)}), bf16[2048,1024]{1,0:T(8,128)(2,1)}) %all-gather.10.cloned.1.call-update) | async-done | bytes 4194320 | tf_op jit(solution)/shard_map/all_gather | solution.py:15
  143.5 4.4 reduce_sum.160
  147.9 3.3 fusion.24
  151.2 2.0 convert_add_fusion.1
  154.5 2.5 fusion.39
  157.1 3.6 convolution_convert_fusion.4
  161.6 6.0 all-gather.1
  170.3 3.6 all-gather.8.cloned.1.call-done
  173.9 10.2 %fusion.35 = f32[16,64,512]{2,1,0:T(8,128)} fusion(bf16[512,16,64]{0,2,1:T(8,128)(2,1)} %bitcast.118, f32[16,512,512]{1,2,0:T(8,128)} %copy-done.1, pred[512,512]{0,1:T(8,128)(4,1)S(1)} %fusion.31), kind=kOutput, calls=%fused_computation.87 | convolution fusion | flops 557842432 | bytes 20185088 | tf_op jit(solution)/shard_map/while/body/eval_jaxpr/hij,ihc->jhc/dot_general | solution.py:46
  184.2 9.8 %fusion.33 = f32[16,64,512]{2,1,0:T(8,128)} fusion(bf16[512,16,64]{0,2,1:T(8,128)(2,1)S(1)} %bitcast.119, f32[16,512,512]{1,2,0:T(8,128)} %copy-done.1, pred[512,512]{0,1:T(8,128)(4,1)S(1)} %fusion.31), kind=kOutput, calls=%fused_computation.85 | convolution fusion | flops 541065216 | bytes 20185088 | tf_op jit(solution)/shard_map/while/body/eval_jaxpr/hij,ihc->jhc/dot_general | solution.py:46
  194.0 9.7 %fusion.32 = f32[16,64,512]{2,1,0:T(8,128)} fusion(f32[16,512,512]{1,2,0:T(8,128)} %copy-done.1, pred[512,512]{0,1:T(8,128)(4,1)S(1)} %fusion.31, bf16[512,16,64]{0,2,1:T(8,128)(2,1)S(1)} %bitcast.120), kind=kOutput, calls=%fused_computation.84 | convolution fusion | flops 542638080 | bytes 20185088 | tf_op jit(solution)/shard_map/while/body/eval_jaxpr/hij,ihc->jhc/dot_general | solution.py:46
  203.7 1.9 fusion.37
  205.6 8.1 fusion.90
  213.7 11.0 %add_select_fusion = f32[16,512,512]{1,2,0:T(8,128)} fusion(f32[16,512,512]{1,2,0:T(8,128)} %fusion.90, bf16[512,16,64]{0,2,1:T(8,128)(2,1)S(1)} %bitcast.128, f32[16,512]{1,0:T(8,128)S(1)} %copy-done.37, pred[512,512]{0,1:T(8,128)(4,1)S(1)} %fusion.31, bf16[512,16,64]{0,2,1:T(8,128)(2,1)S(1)} %bitcast.123), kind=kOutput, calls=%fused_computation.1 | convolution fusion | flops 551026688 | bytes 35946496 | tf_op jit(solution)/shard_map/while/body/eval_jaxpr/ihc,jhc->hij/dot_general | solution.py:46
  224.8 9.0 %fusion.64 = f32[16,69,512]{2,1,0:T(8,128)} fusion(bf16[512,16,69]{0,2,1:T(8,128)(2,1)S(1)} %copy-done.13, f32[16,512,512]{1,2,0:T(8,128)} %add_select_fusion), kind=kOutput, calls=%fused_computation.138 | convolution fusion | flops 583008256 | bytes 20168704 | tf_op jit(solution)/shard_map/while/body/eval_jaxpr/hij,jhf->ihf/dot_general | solution.py:46
  233.8 2.4 copy-done.2
  236.2 3.0 fusion.67
  239.1 9.8 %fusion.62 = f32[16,69,512]{2,1,0:T(8,128)} fusion(bf16[512,16,69]{0,2,1:T(8,128)(2,1)S(1)} %get-tuple-element.138, f32[16,512,512]{1,2,0:T(8,128)} %add_select_fusion), kind=kOutput, calls=%fused_computation.136 | convolution fusion | flops 583008256 | bytes 20168704 | tf_op jit(solution)/shard_map/while/body/eval_jaxpr/hij,ihf->jhf/dot_general | solution.py:46
  249.0 14.8 %fusion.66 = f32[16,69,512]{2,1,0:T(8,128)} fusion(bf16[512,16,69]{0,2,1:T(8,128)(2,1)S(1)} %get-tuple-element.138, f32[16,512,512]{1,2,0:T(8,128)} %add_select_fusion), kind=kOutput, calls=%fused_computation.140 | convolution fusion | flops 595591168 | bytes 20168704 | tf_op jit(solution)/shard_map/while/body/eval_jaxpr/hij,ihf->jhf/dot_general | solution.py:46
  263.8 2.2 fusion.13
  266.0 4.7 broadcast.180.clone
  270.8 11.4 %dynamic_update_slice.34 = f32[512,16,276]{0,2,1:T(8,128)} dynamic-update-slice(f32[512,16,276]{0,2,1:T(8,128)} %broadcast.180.clone, f32[512,16,69]{0,2,1:T(8,128)} %fusion.13, s32[]{:T(128)} %constant.120.clone.1, s32[]{:T(128)} %constant.120.clone.1, s32[]{:T(128)S(6)} %select_n.30) | dynamic-update-slice | bytes 4521988 | tf_op jit(solution)/shard_map/transpose(jvp())/dynamic_update_slice | solution.py:62
  282.2 4.8 slice_multiply_fusion.1
  288.3 5.7 multiply_reduce_fusion.2
  294.0 1.9 add_bitcast_fusion
  295.9 4.7 broadcast.180.clone.1
  300.7 11.4 %dynamic_update_slice.35 = f32[512,16,276]{0,2,1:T(8,128)} dynamic-update-slice(f32[512,16,276]{0,2,1:T(8,128)} %broadcast.180.clone.1, f32[512,16,69]{0,2,1:T(8,128)} %add_bitcast_fusion, s32[]{:T(128)} %constant.120.clone.1, s32[]{:T(128)} %constant.120.clone.1, s32[]{:T(128)S(6)} %select_n.30) | dynamic-update-slice | bytes 4521988 | tf_op jit(solution)/shard_map/transpose(jvp())/dynamic_update_slice | solution.py:62
  312.1 4.8 slice_multiply_fusion
  318.2 5.5 multiply_reduce_fusion
  323.8 2.2 fusion.43
  328.8 2.3 convolution_convert_fusion.2
  332.8 2.3 convolution_convert_fusion.1
  337.0 3.6 convolution_convert_fusion.3
  340.6 2.6 copy.94
  343.3 3.0 convolution_convert_fusion.6
  346.3 2.1 copy.88
  348.5 40.9 %all-reduce.7.cloned.1.call-done = (bf16[512,1024]{1,0:T(8,128)(2,1)}, bf16[512,1024]{0,1:T(8,128)(2,1)}, bf16[512,256]{0,1:T(8,128)(2,1)}, bf16[512,256]{0,1:T(8,128)(2,1)}) async-done(((bf16[512,1024]{1,0:T(8,128)(2,1)}, bf16[512,1024]{0,1:T(8,128)(2,1)}, bf16[512,256]{0,1:T(8,128)(2,1)}, bf16[512,256]{0,1:T(8,128)(2,1)}), (bf16[512,1024]{1,0:T(8,128)(2,1)}, bf16[512,1024]{0,1:T(8,128)(2,1)}, ...) | async-done | bytes 2621456 | tf_op jit(solution)/shard_map/psum | solution.py:233
  389.4 2.4 convolution_convert_fusion.8
  393.4 4.0 convolution_convert_fusion
  399.4 58.6 %reduce-scatter.27.cloned.1.call-done = bf16[128,688]{1,0:T(8,128)(2,1)} async-done(((bf16[1024,688]{1,0:T(8,128)(2,1)}), bf16[128,688]{1,0:T(8,128)(2,1)}) %reduce-scatter.27.cloned.1.call-update) | async-done | bytes 176144
  459.8 65.4 %reduce-scatter.29.cloned.1.call-done = bf16[128,688]{1,0:T(8,128)(2,1)} async-done(((bf16[1024,688]{1,0:T(8,128)(2,1)}), bf16[128,688]{1,0:T(8,128)(2,1)}) %reduce-scatter.29.cloned.1.call-update) | async-done | bytes 176144
  527.0 65.8 %reduce-scatter.31.cloned.1.call-done = bf16[128,688]{1,0:T(8,128)(2,1)} async-done(((bf16[1024,688]{1,0:T(8,128)(2,1)}), bf16[128,688]{1,0:T(8,128)(2,1)}) %reduce-scatter.31.cloned.1.call-update) | async-done | bytes 176144
  594.7 62.3 %reduce-scatter.25.cloned.1.call-done = bf16[128,256]{1,0:T(8,128)(2,1)} async-done(((bf16[1024,256]{1,0:T(8,128)(2,1)}), bf16[128,256]{1,0:T(8,128)(2,1)}) %reduce-scatter.25.cloned.1.call-update) | async-done | bytes 65552
  661.6 2.3 fusion.28
  663.9 19.5 %all-reduce.3 = (bf16[1024]{0:T(1024)(128)(2,1)S(1)}, bf16[1024]{0:T(1024)(128)(2,1)S(1)}) all-reduce(bf16[1024]{0:T(1024)(128)(2,1)S(1)} %get-tuple-element.111, bf16[1024]{0:T(1024)(128)(2,1)S(1)} %copy-done.50), channel_id=5, replica_groups=mesh['dp'=8,'feat'=4] {'dp'}, use_global_device_ids=true, to_apply=%region_20.21.clone | all-reduce | flops 2048 | bytes 8192
  684.0 5.3 fusion.19
  689.3 32.8 %reduce-scatter.19.cloned.1.call-done = bf16[128,256]{1,0:T(8,128)(2,1)} async-done(((bf16[1024,256]{1,0:T(8,128)(2,1)}), bf16[128,256]{1,0:T(8,128)(2,1)}) %reduce-scatter.19.cloned.1.call-update) | async-done | bytes 65552 | tf_op jit(solution)/shard_map/reduce_scatter | solution.py:318
  723.6 62.7 %reduce-scatter.21.cloned.1.call-done = bf16[128,256]{1,0:T(8,128)(2,1)} async-done(((bf16[1024,256]{1,0:T(8,128)(2,1)}), bf16[128,256]{1,0:T(8,128)(2,1)}) %reduce-scatter.21.cloned.1.call-update) | async-done | bytes 65552 | tf_op jit(solution)/shard_map/reduce_scatter | solution.py:321
  787.8 69.1 %reduce-scatter.23.cloned.1.call-done = bf16[128,1024]{1,0:T(8,128)(2,1)} async-done(((bf16[1024,1024]{1,0:T(8,128)(2,1)}), bf16[128,1024]{1,0:T(8,128)(2,1)}) %reduce-scatter.23.cloned.1.call-update) | async-done | bytes 262160 | tf_op jit(solution)/shard_map/reduce_scatter | solution.py:324
  857.0 1.8 convert_element_type.330
  (197 shorter events, 54.4 us)
Async XLA Ops:
  7.2 1.9 copy-start
  7.2 67.9 %reduce-scatter.17.cloned.1.call-start = ((), (), s32[]{:S(2)}) async-start(), calls=%async_computation.8 | async-start | bytes 2621440 | tf_op jit(solution)/shard_map/reduce_scatter | solution.py:214
  9.1 12.8 %copy-start.46 = (f32[512]{0:T(512)}, f32[512]{0:T(512)S(1)}, u32[]{:S(2)}) copy-start(f32[512]{0:T(512)S(1)} %add_rsqrt_fusion.1) | copy-start | bytes 6148
  12.6 2.4 copy-start.57
  12.6 2.8 copy-start.16
  12.6 2.8 copy-start.48
  15.1 6.7 copy-start.51
  23.6 1.4 copy-start.29
  23.6 2.4 copy-start.15
  23.6 2.4 copy-start.38
  27.6 3.1 copy-start.12
  27.6 3.1 copy-start.8
  30.7 5.8 copy-start.1
  40.8 36.2 %copy-start.52 = (s32[4]{0:T(128)S(1)}, s32[4]{0:T(128)}, u32[]{:S(2)}) copy-start(s32[4]{0:T(128)} %copy-done.51) | copy-start | bytes 52
  40.8 53.3 %all-gather.6.cloned.1.call-start = ((), (), s32[]{:S(2)}) async-start(), calls=%async_computation.9 | async-start | bytes 1310720 | tf_op jit(solution)/shard_map/all_gather | solution.py:221
  77.0 66.5 %all-gather.10.cloned.1.call-start = ((), (), s32[]{:S(2)}) async-start(), calls=%async_computation.14 | async-start | bytes 5242880 | tf_op jit(solution)/shard_map/all_gather | solution.py:15
  94.1 3.7 copy-start.42
  97.7 3.1 copy-start.5
  97.7 2.1 copy-start.53
  99.8 1.7 copy-start.54
  101.6 1.7 copy-start.55
  108.8 65.1 %all-gather.8.cloned.1.call-start = ((), (), s32[]{:S(2)}) async-start(), calls=%async_computation.10 | async-start | bytes 1310720 | tf_op jit(solution)/shard_map/all_gather | solution.py:262
  147.9 3.3 copy-start.6
  147.9 3.3 copy-start.23
  147.9 3.3 copy-start.43
  147.9 3.4 copy-start.45
  157.1 232.3 %all-reduce.7.cloned.1.call-start = ((), (), s32[]{:S(2)}) async-start(), calls=%async_computation.19 | async-start | bytes 5242880 | tf_op jit(solution)/shard_map/psum | solution.py:233
  157.1 3.6 copy-start.32
  157.1 3.6 copy-start.33
  173.9 10.2 %copy-start.7 = (bf16[512,1024]{0,1:T(8,128)(2,1)S(1)}, bf16[512,1024]{0,1:T(8,128)(2,1)}, u32[]{:S(2)}) copy-start(bf16[512,1024]{0,1:T(8,128)(2,1)} %all-gather.8.cloned.1.call-done) | copy-start | bytes 3145732
  203.7 1.9 copy-start.9
  205.6 8.1 copy-start.37
  213.7 11.0 %copy-start.13 = (bf16[512,16,69]{0,2,1:T(8,128)(2,1)S(1)}, bf16[512,16,69]{0,2,1:T(8,128)(2,1)}, u32[]{:S(2)}) copy-start(bf16[512,16,69]{0,2,1:T(8,128)(2,1)} %copy-done.12) | copy-start | bytes 3391492
  224.8 11.4 %copy-start.2 = (f32[16,512,512]{1,2,0:T(8,128)S(1)}, f32[16,512,512]{1,2,0:T(8,128)}, u32[]{:S(2)}) copy-start(f32[16,512,512]{1,2,0:T(8,128)} %add_select_fusion) | copy-start | bytes 50331652
  249.0 14.8 %copy-start.20 = (f32[16,69,512]{2,1,0:T(8,128)S(1)}, f32[16,69,512]{2,1,0:T(8,128)}, u32[]{:S(2)}) copy-start(f32[16,69,512]{2,1,0:T(8,128)} %fusion.64) | copy-start | bytes 6782980
  249.0 14.8 %copy-start.21 = (f32[16,69,512]{2,1,0:T(8,128)S(1)}, f32[16,69,512]{2,1,0:T(8,128)}, u32[]{:S(2)}) copy-start(f32[16,69,512]{2,1,0:T(8,128)} %fusion.67) | copy-start | bytes 6782980
  249.0 14.8 %copy-start.22 = (f32[16,69,512]{2,1,0:T(8,128)S(1)}, f32[16,69,512]{2,1,0:T(8,128)}, u32[]{:S(2)}) copy-start(f32[16,69,512]{2,1,0:T(8,128)} %fusion.37) | copy-start | bytes 6782980
  249.0 14.8 %copy-start.41 = (f32[512,16]{0,1:T(8,128)S(1)}, f32[512,16]{0,1:T(8,128)}, u32[]{:S(2)}) copy-start(f32[512,16]{0,1:T(8,128)} %multiply_bitcast_fusion) | copy-start | bytes 98308
  282.2 6.1 copy-start.4
  282.2 6.1 copy-start.30
  288.3 5.7 copy-start.10
  288.3 5.7 copy-start.18
  288.3 5.7 copy-start.19
  312.1 6.1 copy-start.3
  312.1 6.1 copy-start.28
  318.2 8.7 %copy-start.25 = (f32[16,64,512]{2,1,0:T(8,128)S(1)}, f32[16,64,512]{2,1,0:T(8,128)}, u32[]{:S(2)}) copy-start(f32[16,64,512]{2,1,0:T(8,128)} %fusion.33) | copy-start | bytes 6291460
  318.2 8.7 %copy-start.26 = (f32[16,64,512]{2,1,0:T(8,128)S(1)}, f32[16,64,512]{2,1,0:T(8,128)}, u32[]{:S(2)}) copy-start(f32[16,64,512]{2,1,0:T(8,128)} %fusion.32) | copy-start | bytes 6291460
  323.8 3.2 copy-start.14
  323.8 3.1 copy-start.24
  328.7 129.3 %reduce-scatter.27.cloned.1.call-start = ((), (), s32[]{:S(2)}) async-start(), calls=%async_computation.16 | async-start | bytes 1769472
  332.7 192.5 %reduce-scatter.29.cloned.1.call-start = ((), (), s32[]{:S(2)}) async-start(), calls=%async_computation.17 | async-start | bytes 1769472
  336.7 256.1 %reduce-scatter.31.cloned.1.call-start = ((), (), s32[]{:S(2)}) async-start(), calls=%async_computation.18 | async-start | bytes 1769472
  340.6 2.8 copy-start.31
  343.2 46.1 %copy-start.17 = (bf16[512,1024]{1,0:T(8,128)(2,1)S(1)}, bf16[512,1024]{1,0:T(8,128)(2,1)}, u32[]{:S(2)}) copy-start(bf16[512,1024]{1,0:T(8,128)(2,1)} %param.12) | copy-start | bytes 3145732
  343.3 46.1 %copy-start.47 = (f32[512]{0:T(512)S(1)}, f32[512]{0:T(512)}, u32[]{:S(2)}) copy-start(f32[512]{0:T(512)} %copy-done.46) | copy-start | bytes 6148
  343.3 46.1 %copy-start.49 = (f32[1024]{0:T(1024)S(1)}, f32[1024]{0:T(1024)}, u32[]{:S(2)}) copy-start(f32[1024]{0:T(1024)} %param.13) | copy-start | bytes 12292
  343.3 313.7 %reduce-scatter.25.cloned.1.call-start = ((), (), s32[]{:S(2)}) async-start(), calls=%async_computation.15 | async-start | bytes 589824
  348.4 373.7 %reduce-scatter.19.cloned.1.call-start = ((), (), s32[]{:S(2)}) async-start(), calls=%async_computation.11 | async-start | bytes 589824 | tf_op jit(solution)/shard_map/reduce_scatter | solution.py:318
  389.4 2.5 copy-start.39
  391.9 394.4 %reduce-scatter.21.cloned.1.call-start = ((), (), s32[]{:S(2)}) async-start(), calls=%async_computation.12 | async-start | bytes 589824 | tf_op jit(solution)/shard_map/reduce_scatter | solution.py:321
  393.4 463.6 %reduce-scatter.23.cloned.1.call-start = ((), (), s32[]{:S(2)}) async-start(), calls=%async_computation.13 | async-start | bytes 2359296 | tf_op jit(solution)/shard_map/reduce_scatter | solution.py:324
  657.9 2.3 copy-start.56
  660.2 1.3 copy-start.36
  661.6 2.3 copy-start.50
  (10 other events, 9.7 us)
Sparse Core Ops, SparseCore 0:
  41.0 34.1 reduce-scatter.16
  77.3 16.7 all-gather.5
  109.0 34.4 all-gather.9
  157.2 16.7 all-gather.7
  328.8 60.5 all-reduce.6
  393.0 64.8 reduce-scatter.26
  461.4 63.7 reduce-scatter.28
  529.0 63.7 reduce-scatter.30
  596.1 60.7 reduce-scatter.24
  661.1 60.9 reduce-scatter.18
  725.4 60.8 reduce-scatter.20
  790.1 66.8 reduce-scatter.22
